TPU v7x, 32 devices: a whole 2x2x4 slice. The times are simulated.
32 devices in a mesh: dp: 8 (over z, x), node: 4 (over y, core).
Axes of the slice: x: 2, y: 2, z: 4, core: 2. Of those that a mesh axis runs over, the one named last changes fastest.
Arguments:
- inputs: bfloat16 [4352, 12288], P(('dp', 'node')), may hold values from -6 to 6
- norm_gain: bfloat16 [12288], replicated, may hold values from 0.5 to 1.5
- cotangent: bfloat16 [4352, 128], P(('dp', 'node')), may hold values from -6 to 6
- weights: bfloat16 [12288, 128], P('dp', 'node'), may hold values from -6 to 6
- first_moment: bfloat16 [12288, 128], P('dp', 'node'), may hold values from -18 to 18
- second_moment: bfloat16 [12288, 128], P('dp', 'node'), may hold values from 1 to 30
Outputs:
- projected: bfloat16 [4352, 128], P(('dp', 'node'))
- gain_grad: float32 [12288], replicated
- new_weights: bfloat16 [12288, 128], P('dp', 'node')
- new_first: bfloat16 [12288, 128], P('dp', 'node')
- new_second: bfloat16 [12288, 128], P('dp', 'node')
All inputs are finite; a program needn't handle non-finite values.
Results may differ from a plain program's by a relative error of at most 0.0024.
The roundings to bfloat16 on the way count: a program that leaves them out, or rounds other values in their place, can miss the bound.
Values may be sent and summed in bfloat16 or wider, within the bound.
A program may use at most 64 MiB of HBM per device.

v0:
```python
import jax
import jax.numpy as jnp
from jax import lax
from jax.sharding import PartitionSpec as P

STEP = 20


def per_device(inputs, norm_gain, cotangent, weights, first_moment, second_moment):
    width = inputs.shape[1]
    factor = width ** (-0.5)
    rows_in = inputs.astype(jnp.float32)
    inverse = lax.rsqrt(jnp.mean(rows_in * rows_in, axis=1, keepdims=True) + 1e-05)
    scaled = rows_in * inverse
    normed = (scaled * norm_gain.astype(jnp.float32)).astype(jnp.bfloat16)
    secondary = lax.all_gather(weights, "dp", axis=0, tiled=True)
    projected = (
        factor
        * jnp.dot(
            normed,
            lax.all_gather(secondary, "node", axis=1, tiled=True),
            preferred_element_type=jnp.float32,
        )
    ).astype(jnp.bfloat16)
    back = factor * lax.dot_general(
        cotangent,
        lax.all_gather(secondary, "node", axis=1, tiled=True),
        (((1,), (1,)), ((), ())),
        preferred_element_type=jnp.float32,
    )
    gain_grad = lax.psum(jnp.sum(back * scaled, axis=0), ("dp", "node"))
    raw = factor * lax.dot_general(
        normed, cotangent, (((0,), (0,)), ((), ())), preferred_element_type=jnp.float32
    )
    rounded = lax.optimization_barrier(raw.astype(jnp.bfloat16))
    row_sums = lax.psum_scatter(rounded.astype(jnp.float32), "dp", scatter_dimension=0, tiled=True)
    grad = lax.psum_scatter(
        row_sums.astype(jnp.bfloat16), "node", scatter_dimension=1, tiled=True
    ).astype(jnp.float32)
    first = 0.9 * first_moment.astype(jnp.float32) + 0.1 * grad
    second = 0.95 * second_moment.astype(jnp.float32) + 0.05 * grad * grad
    update = first / (1.0 - 0.9**STEP) / (jnp.sqrt(second / (1.0 - 0.95**STEP)) + 1e-08)
    new_weights = (weights.astype(jnp.float32) - 0.05 * update).astype(jnp.bfloat16)
    return (
        projected,
        gain_grad,
        new_weights,
        first.astype(jnp.bfloat16),
        second.astype(jnp.bfloat16),
    )


def solution(mesh):
    return jax.shard_map(
        per_device,
        mesh=mesh,
        in_specs=(
            P(("dp", "node"), None),
            P(),
            P(("dp", "node"), None),
            P("dp", "node"),
            P("dp", "node"),
            P("dp", "node"),
        ),
        out_specs=(P(("dp", "node"), None), P(), P("dp", "node"), P("dp", "node"), P("dp", "node")),
        check_vma=False,
    )
```

profile of v0, /device:TPU:0, one launch (start us, length us, event | category | flops | bytes accessed | tf_op | source)
XLA Modules:
  0.0 158.9 jit_solution(6191956120194625562)
XLA Ops:
  8.0 0.0 copy-start
  8.0 0.0 copy-start.1
  8.0 0.0 reduce-scatter.5.cloned.1.call-start
  8.1 0.9 convert_element_type.43
  9.0 2.8 %fusion.4 = f32[136]{0:T(256)S(1)} fusion(bf16[136,12288]{1,0:T(8,128)(2,1)} %param.6), kind=kLoop, calls=%fused_computation.8 | loop fusion | flops 5013368 | bytes 3342880 | tf_op jit(solution)/shard_map/reduce_sum | solution.py:13
  11.8 0.0 copy-done
  11.8 0.0 copy-done.1
  11.8 0.0 copy-start.2
  11.8 3.7 %fusion.1 = bf16[12288,128]{1,0:T(8,128)(2,1)} fusion(bf16[136,128]{1,0:T(8,128)(2,1)S(1)} %copy-done, bf16[136,12288]{1,0:T(8,128)(2,1)S(1)} %copy-done.1, f32[12288]{0:T(1024)S(1)} %convert_element_type.43, f32[136]{0:T(256)S(1)} %add_rsqrt_fusion), kind=kOutput, calls=%fused_computation.3 | convolution fusion | flops 437649408 | bytes 6572576 | tf_op jit(solution)/shard_map/dot_general | solution.py:32
  15.5 0.0 reduce-scatter.5.cloned.1.call-update
  15.5 0.0 all-gather.2.cloned.1.call-start
  15.6 0.0 copy-done.2
  15.6 38.1 %all_gather.7 = bf16[12288,32]{0,1:T(8,128)(2,1)} all-gather(bf16[1536,32]{0,1:T(8,128)(2,1)S(1)} %copy-done.2), channel_id=1, replica_groups=mesh['dp'=8,'node'=4] {'dp'}, dimensions={0}, use_global_device_ids=true | all-gather | bytes 884736 | tf_op jit(solution)/shard_map/all_gather | solution.py:16
  53.7 0.0 all-gather.2.cloned.1.call-update
  53.8 0.0 reduce-scatter.7.cloned.1.call-start
  53.8 44.9 %reduce-scatter.5.cloned.1.call-done = bf16[1536,128]{1,0:T(8,128)(2,1)} async-done(((bf16[12288,128]{1,0:T(8,128)(2,1)}), bf16[1536,128]{1,0:T(8,128)(2,1)}) %reduce-scatter.5.cloned.1.call-update) | async-done | bytes 393232 | tf_op jit(solution)/shard_map/reduce_scatter | solution.py:36
  98.7 1.9 %copy.24 = bf16[1536,128]{0,1:T(8,128)(2,1)} copy(bf16[1536,128]{1,0:T(8,128)(2,1)} %reduce-scatter.5.cloned.1.call-done) | data formatting | bytes 786432
  100.6 0.0 reduce-scatter.7.cloned.1.call-update
  100.6 0.0 all-gather.2.cloned.1.call-done
  100.7 4.3 %fusion.5 = f32[12288]{0:T(1024)} fusion(f32[136]{0:T(256)S(1)} %add_rsqrt_fusion, bf16[136,12288]{1,0:T(8,128)(2,1)S(1)} %copy-done.1, bf16[136,128]{1,0:T(8,128)(2,1)S(1)} %copy-done, bf16[12288,128]{0,1:T(8,128)(2,1)} %all-gather.2.cloned.1.call-done), kind=kOutput, calls=%fused_computation.9 | convolution fusion | flops 436162560 | bytes 6572576 | tf_op jit(solution)/shard_map/dot_general | solution.py:25
  105.0 40.6 %psum.7 = f32[12288]{0:T(1024)} all-reduce(f32[12288]{0:T(1024)} %fusion.5), channel_id=1, replica_groups=mesh['dp'=8,'node'=4] {'dp','node'}, use_global_device_ids=true, to_apply=%region_2.0 | all-reduce | flops 12288 | bytes 98304 | tf_op jit(solution)/shard_map/psum | solution.py:31
  145.6 4.0 %fusion.6 = bf16[136,128]{1,0:T(8,128)(2,1)} fusion(bf16[12288,128]{0,1:T(8,128)(2,1)} %all-gather.2.cloned.1.call-done, bf16[136,12288]{1,0:T(8,128)(2,1)S(1)} %copy-done.1, f32[12288]{0:T(1024)S(1)} %convert_element_type.43, f32[136]{0:T(256)S(1)} %add_rsqrt_fusion), kind=kOutput, calls=%fused_computation.11 | convolution fusion | flops 434538496 | bytes 6572576 | tf_op jit(solution)/shard_map/dot_general | solution.py:19
  149.6 0.0 reduce-scatter.7.cloned.1.call-done
  149.6 1.9 %fusion.12 = (bf16[1536,32]{0,1:T(8,128)(2,1)}, bf16[1536,32]{0,1:T(8,128)(2,1)}, bf16[1536,32]{0,1:T(8,128)(2,1)}) fusion(bf16[1536,32]{0,1:T(8,128)(2,1)} %param.11, bf16[32,1536]{1,0:T(8,128)(2,1)} %reduce-scatter.7.cloned.1.call-done, bf16[1536,32]{0,1:T(8,128)(2,1)} %param.10, bf16[1536,32]{0,1:T(8,128)(2,1)S(1)} %copy-done.2), kind=kLoop, calls=%fused_computation.18 | loop fusion | flops 983040 | bytes 688128 | tf_op jit(solution)/shard_map/convert_element_type | solution.py:49
  (1 shorter events, 0.0 us)
Async XLA Ops:
  8.0 3.8 %copy-start = (bf16[136,128]{1,0:T(8,128)(2,1)S(1)}, bf16[136,128]{1,0:T(8,128)(2,1)}, u32[]{:S(2)}) copy-start(bf16[136,128]{1,0:T(8,128)(2,1)} %param.8) | copy-start | bytes 104452
  8.0 3.8 %copy-start.1 = (bf16[136,12288]{1,0:T(8,128)(2,1)S(1)}, bf16[136,12288]{1,0:T(8,128)(2,1)}, u32[]{:S(2)}) copy-start(bf16[136,12288]{1,0:T(8,128)(2,1)} %param.6) | copy-start | bytes 10027012
  8.0 90.7 %reduce-scatter.5.cloned.1.call-start = ((), (), s32[]{:S(2)}) async-start(), calls=%async_computation.3 | async-start | bytes 3538944 | tf_op jit(solution)/shard_map/reduce_scatter | solution.py:36
  11.8 3.8 %copy-start.2 = (bf16[1536,32]{0,1:T(8,128)(2,1)S(1)}, bf16[1536,32]{0,1:T(8,128)(2,1)}, u32[]{:S(2)}) copy-start(bf16[1536,32]{0,1:T(8,128)(2,1)} %param.9) | copy-start | bytes 294916
  15.5 85.1 %all-gather.2.cloned.1.call-start = ((), (), s32[]{:S(2)}) async-start(), calls=%async_computation.2 | async-start | bytes 3932160 | tf_op jit(solution)/shard_map/all_gather | solution.py:21
  53.8 95.8 %reduce-scatter.7.cloned.1.call-start = ((), (), s32[]{:S(2)}) async-start(), calls=%async_computation.4 | async-start | bytes 491520
Sparse Core Ops, SparseCore 0:
  15.7 83.0 reduce-scatter.4
Sparse Core Ops, SparseCore 1:
  53.9 29.4 all-gather.1
  100.7 19.9 reduce-scatter.6
where the time goes:
time: 159 us
  blocking collectives  78.7 us (49%)
  waiting for transfers between devices  45 us (28%)
  between operations  15.5 us (10%)
  matrix products  12 us (8%)
  other arithmetic  5.57 us (4%)
  local copies, waits for them, and re-layouts  1.93 us (1%)
    reduce_scatter x1, waiting for transfers between devices, per_device(): lax.psum_scatter(rounded.astype(jnp.float32), 'dp', scatter_dimension=0,...  44.9 us
    psum x1, blocking collectives, per_device(): gain_grad = lax.psum(jnp.sum(back * scaled, axis=0), ('dp', 'node'))  40.6 us
    all_gather x1, blocking collectives, per_device(): secondary = lax.all_gather(weights, 'dp', axis=0, tiled=True)  38.1 us
    dot_general x1, matrix products, per_device(): lax.dot_general(cotangent, lax.all_gather(secondary, 'node', axis=1, tile...  4.33 us
    dot_general x1, matrix products, per_device(): jnp.dot(normed, lax.all_gather(secondary, 'node', axis=1, tiled=True), pr...  3.95 us
    dot_general x1, matrix products, per_device(): lax.dot_general(normed, cotangent, (((0,), (0,)), ((), ())), preferred_el...  3.72 us
  transfers between devices with their start and end apart: 3, of which 1 were waited for; matrix products, arithmetic and copies ran while one was open for 6% of the time, Pallas kernels for 0%

commit v1 on v0

v1 whole, which is shorter than its diff:
```python
import functools

import jax
import jax.numpy as jnp
from jax import lax
from jax.experimental import pallas as pl
from jax.experimental.pallas import tpu as pltpu
from jax.sharding import PartitionSpec as P

STEP = 20
MESH = pl.DeviceIdType.MESH
F32 = jnp.float32
BF16 = jnp.bfloat16


def adam(grad, weights, first_moment, second_moment):
    first = 0.9 * first_moment.astype(F32) + 0.1 * grad
    second = 0.95 * second_moment.astype(F32) + 0.05 * grad * grad
    update = first / (1.0 - 0.9**STEP) / (jnp.sqrt(second / (1.0 - 0.95**STEP)) + 1e-08)
    new_weights = (weights.astype(F32) - 0.05 * update).astype(BF16)
    return new_weights, first.astype(BF16), second.astype(BF16)


def plain(inputs, norm_gain, cotangent, weights, first_moment, second_moment):
    width = inputs.shape[1]
    factor = width ** (-0.5)
    rows_in = inputs.astype(F32)
    inverse = lax.rsqrt(jnp.mean(rows_in * rows_in, axis=1, keepdims=True) + 1e-05)
    scaled = rows_in * inverse
    normed = (scaled * norm_gain.astype(F32)).astype(BF16)
    secondary = lax.all_gather(weights, "dp", axis=0, tiled=True)
    whole = lax.all_gather(secondary, "node", axis=1, tiled=True)
    projected = (factor * jnp.dot(normed, whole, preferred_element_type=F32)).astype(BF16)
    back = factor * lax.dot_general(
        cotangent, whole, (((1,), (1,)), ((), ())), preferred_element_type=F32
    )
    gain_grad = lax.psum(jnp.sum(back * scaled, axis=0), ("dp", "node"))
    raw = factor * lax.dot_general(
        normed, cotangent, (((0,), (0,)), ((), ())), preferred_element_type=F32
    )
    rounded = lax.optimization_barrier(raw.astype(BF16))
    row_sums = lax.psum_scatter(rounded.astype(F32), "dp", scatter_dimension=0, tiled=True)
    grad = lax.psum_scatter(row_sums.astype(BF16), "node", scatter_dimension=1, tiled=True).astype(F32)
    return (projected, gain_grad) + adam(grad, weights, first_moment, second_moment)


def kernel(
    nz, x_ref, gain_ref, cot_ref, w_ref, m1_ref, m2_ref,
    proj_ref, gg_ref, nw_ref, n1_ref, n2_ref,
    G, T, RC, S1, RY, XS, RX, ZS, RZ, OWN, NORM, RSTD, ACC, GA, GB, GR, GZ,
    gy_s, gy_r, gz_s, gz_r, gx_s, gx_r, gc_s, gc_r,
    rc_s, rc_r, ry_s, ry_r, rx_s, rx_r, rz_s, rz_r, ga_s, ga_r,
):
    tok, width = x_ref.shape
    cols, rows = w_ref.shape
    factor = width ** (-0.5)
    chunks = 2 * nz
    dp, node = lax.axis_index("dp"), lax.axis_index("node")
    z, x = dp // 2, lax.rem(dp, 2)
    y, c = node // 2, lax.rem(node, 2)
    core_dev = (dp, y * 2 + 1 - c)
    y_dev = (dp, (1 - y) * 2 + c)
    x_dev = (z * 2 + 1 - x, node)
    z_to = [lax.rem(z + 1 + j, nz) for j in range(nz)]
    z_from = [lax.rem(z + nz - 1 - j, nz) for j in range(nz)]
    z_dev = [(z_to[j] * 2 + x, node) for j in range(nz - 1)]

    sends = []

    def copy(src, dst, s, r, dev):
        return pltpu.make_async_remote_copy(
            src_ref=src, dst_ref=dst, send_sem=s, recv_sem=r, device_id=dev, device_id_type=MESH
        )

    def send(*a):
        d = copy(*a)
        d.start()
        sends.append(d)

    def arrived(dst, s, r, dev):
        copy(dst, dst, s, r, dev).wait_recv()

    barrier = pltpu.get_barrier_semaphore()
    partners = [core_dev, y_dev, x_dev] + z_dev
    for dev in partners:
        pl.semaphore_signal(barrier, inc=1, device_id=dev, device_id_type=MESH)
    pl.semaphore_wait(barrier, len(partners))

    send(w_ref, G.at[c, x, z, y], gy_s, gy_r, y_dev)
    G[c, x, z, y] = w_ref[...]

    square = jnp.zeros((tok, 128), F32)
    for k in range(width // 128):
        v = x_ref[:, k * 128 : (k + 1) * 128].astype(F32)
        square = square + v * v
    RSTD[...] = lax.rsqrt(jnp.sum(square, axis=1, keepdims=True) / width + 1e-05)

    arrived(G.at[c, x, z, 1 - y], gy_s, gy_r, y_dev)
    mine = G.at[c, x, z]
    for j in reversed(range(nz - 1)):
        send(mine, mine, gz_s.at[j], gz_r.at[j], z_dev[j])
    send(mine, mine, gx_s.at[nz - 1], gx_r.at[nz - 1], x_dev)
    send(mine, mine, gc_s.at[nz - 1], gc_r.at[nz - 1], core_dev)

    half = 2 * cols
    a = lax.broadcasted_iota(jnp.int32, (4 * cols, 4 * cols), 0)
    b = lax.broadcasted_iota(jnp.int32, (4 * cols, 4 * cols), 1)
    source = (lax.rem(b, half) // cols) * half + (b // half) * cols + lax.rem(b, cols)
    perm = jnp.where(a == source, 1.0, 0.0).astype(BF16)
    cot = jnp.dot(cot_ref[...], perm, preferred_element_type=F32).astype(BF16)
    cot_t = cot.T

    def place(k):
        xk = 1 - x if k < nz else x
        return xk, z_to[k % nz]

    def lanes(xk, zk):
        return pl.ds(pl.multiple_of((zk * 2 + xk) * rows, 128), rows)

    def stage_term(k):
        xk, zk = place(k)
        at = lanes(xk, zk)
        scaled = x_ref[:, at].astype(F32) * RSTD[...]
        normed = (scaled * gain_ref[:, at].astype(F32)).astype(BF16)
        NORM[zk * 2 + xk] = normed
        term = (factor * jnp.dot(cot_t, normed, preferred_element_type=F32)).astype(BF16)
        T[k, 0] = term[:half].reshape(2, cols, rows)
        T[k, 1] = term[half:].reshape(2, cols, rows)
        send(T.at[k, 1 - c], RC.at[k], rc_s.at[k], rc_r.at[k], core_dev)

    def stage_core(k):
        arrived(RC.at[k], rc_s.at[k], rc_r.at[k], core_dev)
        S1[k] = (T[k, c].astype(F32) + RC[k].astype(F32)).astype(BF16)
        send(S1.at[k, 1 - y], RY.at[k], ry_s.at[k], ry_r.at[k], y_dev)

    def stage_y(k):
        arrived(RY.at[k], ry_s.at[k], ry_r.at[k], y_dev)
        total = S1[k, y].astype(F32) + RY[k].astype(F32)
        if k < nz:
            XS[k] = total.astype(BF16)
            send(XS.at[k], RX.at[k], rx_s.at[k], rx_r.at[k], x_dev)
            return
        j = k - nz
        arrived(RX.at[j], rx_s.at[j], rx_r.at[j], x_dev)
        total = total + RX[j].astype(F32)
        if j < nz - 1:
            ZS[j] = total.astype(BF16)
            send(ZS.at[j], RZ.at[j], rz_s.at[j], rz_r.at[j], z_dev[j])
        else:
            OWN[...] = total

    def forward_z(j):
        block = G.at[c, x, z_from[j]]
        arrived(block, gz_s.at[j], gz_r.at[j], z_dev[j])
        send(block, block, gx_s.at[j], gx_r.at[j], x_dev)
        send(block, block, gc_s.at[j], gc_r.at[j], core_dev)

    def forward_x(j):
        block = G.at[c, 1 - x, z_from[j]]
        arrived(block, gx_s.at[j], gx_r.at[j], x_dev)
        send(block, block, gc_s.at[nz + j], gc_r.at[nz + j], core_dev)

    def use(i):
        j = i % nz
        xk, zk = (x if i < nz else 1 - x), z_from[j]
        arrived(G.at[1 - c, xk, zk], gc_s.at[i], gc_r.at[i], core_dev)
        at = lanes(xk, zk)
        wt = jnp.concatenate(
            [G[0, xk, zk].reshape(half, rows), G[1, xk, zk].reshape(half, rows)], axis=0
        )
        part = lax.dot_general(
            NORM[zk * 2 + xk], wt, (((1,), (1,)), ((), ())), preferred_element_type=F32
        )
        ACC[...] += part
        back = factor * jnp.dot(cot, wt, preferred_element_type=F32)
        scaled = x_ref[:, at].astype(F32) * RSTD[...]
        GA[pl.ds(zk * 2 + xk, 1), :] = jnp.sum(back * scaled, axis=0, keepdims=True)

    ACC[...] = jnp.zeros_like(ACC)
    for k in range(chunks):
        stage_term(k)
        if k >= 1:
            stage_core(k - 1)
    stage_core(chunks - 1)
    stage_y(0)
    stage_y(1)
    use(nz - 1)
    forward_x(nz - 1)
    done = 2
    for j in reversed(range(nz - 1)):
        stage_y(done)
        forward_z(j)
        use(nz + nz - 1) if j == nz - 2 else forward_x(j + 1)
        done += 1
    for j in reversed(range(nz - 1)):
        if done < chunks:
            stage_y(done)
            done += 1
        use(j)
    forward_x(0)
    while done < chunks:
        stage_y(done)
        done += 1
    for j in reversed(range(nz - 1)):
        use(nz + j)

    send(GA, GR.at[0], ga_s.at[0], ga_r.at[0], core_dev)
    out = lax.dot_general(
        (factor * ACC[...]).astype(BF16), perm, (((1,), (1,)), ((), ())), preferred_element_type=F32
    )
    proj_ref[...] = out.astype(BF16)
    arrived(GR.at[0], ga_s.at[0], ga_r.at[0], core_dev)
    GB[0] = GA[...] + GR[0]
    send(GB.at[0], GR.at[1], ga_s.at[1], ga_r.at[1], y_dev)
    arrived(GR.at[1], ga_s.at[1], ga_r.at[1], y_dev)
    GB[1] = GB[0] + GR[1]
    send(GB.at[1], GR.at[2], ga_s.at[2], ga_r.at[2], x_dev)
    arrived(GR.at[2], ga_s.at[2], ga_r.at[2], x_dev)
    GZ[z] = GB[1] + GR[2]
    for j in range(nz - 1):
        send(GZ.at[z], GZ.at[z], ga_s.at[3 + j], ga_r.at[3 + j], z_dev[j])

    grad = OWN[...]
    for j in range(nz - 1):
        arrived(RZ.at[j], rz_s.at[j], rz_r.at[j], z_dev[j])
        grad = grad + RZ[j].astype(F32)
    nw_ref[...], n1_ref[...], n2_ref[...] = adam(grad, w_ref[...], m1_ref[...], m2_ref[...])

    for j in range(nz - 1):
        arrived(GZ.at[z_from[j]], ga_s.at[3 + j], ga_r.at[3 + j], z_dev[j])
    total = GZ[0]
    for j in range(1, nz):
        total = total + GZ[j]
    gg_ref[...] = total
    for d in sends:
        d.wait_send()


def per_device(nz, inputs, norm_gain, cotangent, weights, first_moment, second_moment):
    tok, width = inputs.shape
    rows, cols = weights.shape
    chunks = 2 * nz
    vm = pl.BlockSpec(memory_space=pltpu.VMEM)
    dma = lambda *n: pltpu.SemaphoreType.DMA(n)
    sd = jax.ShapeDtypeStruct
    block = (cols, rows)
    outs = pl.pallas_call(
        functools.partial(kernel, nz),
        out_shape=(
            sd((tok, 4 * cols), BF16),
            sd((chunks, rows), F32),
            sd(block, BF16),
            sd(block, BF16),
            sd(block, BF16),
        ),
        in_specs=[vm] * 6,
        out_specs=(vm,) * 5,
        scratch_shapes=[
            pltpu.VMEM((2, 2, nz, 2) + block, BF16),
            pltpu.VMEM((chunks, 2, 2) + block, BF16),
            pltpu.VMEM((chunks, 2) + block, BF16),
            pltpu.VMEM((chunks, 2) + block, BF16),
            pltpu.VMEM((chunks,) + block, BF16),
            pltpu.VMEM((nz,) + block, BF16),
            pltpu.VMEM((nz,) + block, BF16),
            pltpu.VMEM((nz - 1,) + block, BF16),
            pltpu.VMEM((nz - 1,) + block, BF16),
            pltpu.VMEM(block, F32),
            pltpu.VMEM((chunks, tok, rows), BF16),
            pltpu.VMEM((tok, 1), F32),
            pltpu.VMEM((tok, 4 * cols), F32),
            pltpu.VMEM((chunks, rows), F32),
            pltpu.VMEM((2, chunks, rows), F32),
            pltpu.VMEM((3, chunks, rows), F32),
            pltpu.VMEM((nz, chunks, rows), F32),
            pltpu.SemaphoreType.DMA, pltpu.SemaphoreType.DMA,
            dma(nz - 1), dma(nz - 1), dma(nz), dma(nz), dma(chunks), dma(chunks),
            dma(chunks), dma(chunks), dma(chunks), dma(chunks),
            dma(nz), dma(nz), dma(nz - 1), dma(nz - 1), dma(nz + 2), dma(nz + 2),
        ],
        compiler_params=pltpu.CompilerParams(
            collective_id=0, has_side_effects=True, vmem_limit_bytes=56 * 2**20
        ),
    )(inputs, norm_gain.reshape(1, width), cotangent, weights.T, first_moment.T, second_moment.T)
    projected, gain_grad, new_weights, first, second = outs
    return projected, gain_grad.reshape(width), new_weights.T, first.T, second.T


def solution(mesh):
    dp, node = mesh.shape["dp"], mesh.shape["node"]

    def body(inputs, norm_gain, cotangent, weights, first_moment, second_moment):
        args = (inputs, norm_gain, cotangent, weights, first_moment, second_moment)
        rows, cols = weights.shape
        if node == 4 and dp in (4, 6, 8) and rows % 128 == 0 and cols % 16 == 0:
            return per_device(dp // 2, *args)
        return plain(*args)

    return jax.shard_map(
        body,
        mesh=mesh,
        in_specs=(
            P(("dp", "node"), None),
            P(),
            P(("dp", "node"), None),
            P("dp", "node"),
            P("dp", "node"),
            P("dp", "node"),
        ),
        out_specs=(P(("dp", "node"), None), P(), P("dp", "node"), P("dp", "node"), P("dp", "node")),
        check_vma=False,
    )
```

time: 159 us -> 64.2 us (0.40)
  blocking collectives: 78.7 us -> 0 us
  Pallas kernels: 0 us -> 54.4 us
  waiting for transfers between devices: 45 us -> 0 us
  between operations: 15.5 us -> 0.64 us
  matrix products: 12 us -> 0 us
  local copies, waits for them, and re-layouts: 1.93 us -> 8.8 us
  other arithmetic: 5.57 us -> 0 us
    pallas_call x0 -> x1, Pallas kernels: none -> 54.4 us  [per_device(): pl.pallas_call(functools.partial(kernel, nz), out_shape=(sd((tok, 4 * col...]
    reduce_scatter x1 -> x0, waiting for transfers between devices: 44.9 us -> none  [per_device(): lax.psum_scatter(rounded.astype(jnp.float32), 'dp', scatter_dimension=0,...]
    psum x1 -> x0, blocking collectives: 40.6 us -> none  [per_device(): gain_grad = lax.psum(jnp.sum(back * scaled, axis=0), ('dp', 'node'))]
    all_gather x1 -> x0, blocking collectives: 38.1 us -> none  [per_device(): secondary = lax.all_gather(weights, 'dp', axis=0, tiled=True)]
    dot_general x3 -> x0, matrix products: 12 us -> none  [the longest x1 4.33 us: per_device(): lax.dot_general(cotangent, lax.all_gather(secondary, 'node', axis=1, tile...]
    unnamed x7 -> x4, local copies, waits for them, and re-layouts: 1.93 us -> 6 us
    reshape x0 -> x2, local copies, waits for them, and re-layouts: none -> 2.81 us  [the longest x1 1.42 us: per_device(): gain_grad.reshape(width)]
    reduce_sum x1 -> x0, other arithmetic: 2.79 us -> none  [per_device(): jnp.mean(rows_in * rows_in, axis=1, keepdims=True) + 1e-05]
  transfers between devices with their start and end apart: 3 -> 0, of which waited for: 1 -> 0; matrix products, arithmetic and copies ran while one was open for 6% -> 0% of each run, Pallas kernels for 0% -> 0%
where the time goes in v1:
time: 64.2 us; the launch traced here: 63.8 us
  Pallas kernels  54.4 us (85%)
  local copies, waits for them, and re-layouts  8.8 us (14%)
    pallas_call x1, Pallas kernels, per_device(): pl.pallas_call(functools.partial(kernel, nz), out_shape=(sd((tok, 4 * col...  54.4 us
    unnamed x4, local copies, waits for them, and re-layouts  6 us
    reshape x1, local copies, waits for them, and re-layouts, per_device(): gain_grad.reshape(width)  1.42 us
    reshape x1, local copies, waits for them, and re-layouts, per_device(): norm_gain.reshape(1, width)  1.38 us

profile of v1, /device:TPU:0, one launch (start us, length us, event | category | flops | bytes accessed | tf_op | source)
XLA Modules:
  0.0 63.8 jit_solution(15749431653942452146)
XLA Ops:
  0.6 1.4 %reshape.16.gain_ref = bf16[1,12288]{1,0:T(2,128)(2,1)} reshape(bf16[12288]{0:T(1024)(128)(2,1)} %param.7) | data formatting | bytes 49152 | tf_op jit(solution)/shard_map/reshape | solution.py:284
  2.0 54.4 %shard_map.101 = (bf16[136,128]{1,0:T(8,128)(2,1)}, f32[8,1536]{1,0:T(8,128)}, bf16[32,1536]{1,0:T(8,128)(2,1)}, bf16[32,1536]{1,0:T(8,128)(2,1)}, bf16[32,1536]{1,0:T(8,128)(2,1)}) custom-call(bf16[136,12288]{1,0:T(8,128)(2,1)} %x_ref.1, bf16[1,12288]{1,0:T(2,128)(2,1)} %reshape.16.gain_ref, bf16[136,128]{1,0:T(8,128)(2,1)} %cot_ref.1, ...), custom_call_target="tpu_custom_call" | custom-call | tf_op jit(solution)/shard_map/pallas_call | solution.py:247
  56.4 1.4 %reshape.17 = f32[12288]{0:T(1024)} reshape(f32[8,1536]{1,0:T(8,128)} %get-tuple-element.11) | data formatting | bytes 98304 | tf_op jit(solution)/shard_map/reshape | solution.py:286
  57.8 1.4 %copy.15 = bf16[136,128]{1,0:T(8,128)(2,1)} copy(bf16[136,128]{1,0:T(8,128)(2,1)} %get-tuple-element.20) | data formatting | bytes 69632
  59.2 1.5 %copy.16 = bf16[1536,32]{0,1:T(8,128)(2,1)} copy(bf16[1536,32]{0,1:T(8,128)(2,1)} %bitcast.8) | data formatting | bytes 196608
  60.8 1.5 %copy.17 = bf16[1536,32]{0,1:T(8,128)(2,1)} copy(bf16[1536,32]{0,1:T(8,128)(2,1)} %bitcast.7) | data formatting | bytes 196608
  62.3 1.5 %copy.18 = bf16[1536,32]{0,1:T(8,128)(2,1)} copy(bf16[1536,32]{0,1:T(8,128)(2,1)} %bitcast.6) | data formatting | bytes 196608

commit v2 on v1

--- a/solution.py
+++ b/solution.py
@@ -8,6 +8,8 @@
 from jax.sharding import PartitionSpec as P
 
 STEP = 20
+ORDER = "yzxc"
+PLAN = "TTCP" + "TCYP" * 6 + "CP" + "YPPP" * 8
 MESH = pl.DeviceIdType.MESH
 F32 = jnp.float32
 BF16 = jnp.bfloat16
@@ -45,11 +47,11 @@
 
 
 def kernel(
-    nz, x_ref, gain_ref, cot_ref, w_ref, m1_ref, m2_ref,
-    proj_ref, gg_ref, nw_ref, n1_ref, n2_ref,
-    G, T, RC, S1, RY, XS, RX, ZS, RZ, OWN, NORM, RSTD, ACC, GA, GB, GR, GZ,
-    gy_s, gy_r, gz_s, gz_r, gx_s, gx_r, gc_s, gc_r,
-    rc_s, rc_r, ry_s, ry_r, rx_s, rx_r, rz_s, rz_r, ga_s, ga_r,
+    nz, x_ref, gain_ref, cot_ref, w_ref,
+    proj_ref, gg_ref, grad_ref,
+    GF, G, T, RC, S1, RY, XS, RX, ZS, RZ, OWN, NORM, RSTD, ACC, GA, GB, GR, GZ,
+    g_s, g_r,
+    rc_s, rc_r, ry_s, ry_r, rx_s, rx_r, rz_s, rz_r, ga_s, ga_r, gt_s, gt_r, gb_s, gb_r,
 ):
     tok, width = x_ref.shape
     cols, rows = w_ref.shape
@@ -81,26 +83,45 @@
         copy(dst, dst, s, r, dev).wait_recv()
 
     barrier = pltpu.get_barrier_semaphore()
-    partners = [core_dev, y_dev, x_dev] + z_dev
+    group = []
+    for q in range(1, 8):
+        xq, yq, cq = lax.rem(x + q // 4, 2), lax.rem(y + q // 2 % 2, 2), lax.rem(c + q % 2, 2)
+        group.append(((z * 2 + xq, yq * 2 + cq), xq * 4 + yq * 2 + cq))
+    partners = [dev for dev, _ in group] + z_dev
     for dev in partners:
         pl.semaphore_signal(barrier, inc=1, device_id=dev, device_id_type=MESH)
     pl.semaphore_wait(barrier, len(partners))
 
-    send(w_ref, G.at[c, x, z, y], gy_s, gy_r, y_dev)
+    size = dict(z=nz, x=2, y=2, c=2)
+    here = dict(z=z, x=x, y=y, c=c)
+    waiting, have = [], {}
+
+    def block(o):
+        p = {d: lax.rem(here[d] + o[d], size[d]) for d in size}
+        return G.at[p["c"], p["x"], p["z"], p["y"]]
+
+    def hand_on(o, axes, src):
+        for i, d in enumerate(axes):
+            for j in reversed(range(1, size[d])):
+                n = left.pop(0)
+                dev = {"z": z_dev[j - 1] if d == "z" else None, "x": x_dev, "y": y_dev, "c": core_dev}[d]
+                send(src, block(o), g_s.at[n], g_r.at[n], dev)
+                waiting.append((dict(o, **{d: (o[d] - j) % size[d]}), axes[i + 1 :], n, dev))
+
+    left = list(range(4 * chunks - 1))
+    zero = dict(z=0, x=0, y=0, c=0)
+    hand_on(zero, ORDER, w_ref)
     G[c, x, z, y] = w_ref[...]
+    have[0, 0] = 1
+    gains = gain_ref[...].astype(F32)
+    for r in range(width // 128):
+        GF[:, r * 128 : (r + 1) * 128] = gains[r : r + 1, :]
 
     square = jnp.zeros((tok, 128), F32)
     for k in range(width // 128):
         v = x_ref[:, k * 128 : (k + 1) * 128].astype(F32)
         square = square + v * v
     RSTD[...] = lax.rsqrt(jnp.sum(square, axis=1, keepdims=True) / width + 1e-05)
-
-    arrived(G.at[c, x, z, 1 - y], gy_s, gy_r, y_dev)
-    mine = G.at[c, x, z]
-    for j in reversed(range(nz - 1)):
-        send(mine, mine, gz_s.at[j], gz_r.at[j], z_dev[j])
-    send(mine, mine, gx_s.at[nz - 1], gx_r.at[nz - 1], x_dev)
-    send(mine, mine, gc_s.at[nz - 1], gc_r.at[nz - 1], core_dev)
 
     half = 2 * cols
     a = lax.broadcasted_iota(jnp.int32, (4 * cols, 4 * cols), 0)
@@ -121,7 +142,7 @@
         xk, zk = place(k)
         at = lanes(xk, zk)
         scaled = x_ref[:, at].astype(F32) * RSTD[...]
-        normed = (scaled * gain_ref[:, at].astype(F32)).astype(BF16)
+        normed = (scaled * GF[:, at]).astype(BF16)
         NORM[zk * 2 + xk] = normed
         term = (factor * jnp.dot(cot_t, normed, preferred_element_type=F32)).astype(BF16)
         T[k, 0] = term[:half].reshape(2, cols, rows)
@@ -149,21 +170,16 @@
         else:
             OWN[...] = total
 
-    def forward_z(j):
-        block = G.at[c, x, z_from[j]]
-        arrived(block, gz_s.at[j], gz_r.at[j], z_dev[j])
-        send(block, block, gx_s.at[j], gx_r.at[j], x_dev)
-        send(block, block, gc_s.at[j], gc_r.at[j], core_dev)
-
-    def forward_x(j):
-        block = G.at[c, 1 - x, z_from[j]]
-        arrived(block, gx_s.at[j], gx_r.at[j], x_dev)
-        send(block, block, gc_s.at[nz + j], gc_r.at[nz + j], core_dev)
-
-    def use(i):
-        j = i % nz
-        xk, zk = (x if i < nz else 1 - x), z_from[j]
-        arrived(G.at[1 - c, xk, zk], gc_s.at[i], gc_r.at[i], core_dev)
+    def pump():
+        o, axes, n, dev = waiting.pop(0)
+        arrived(block(o), g_s.at[n], g_r.at[n], dev)
+        hand_on(o, axes, block(o))
+        key = o["x"], o["z"]
+        have[key] = have.get(key, 0) + 1
+        if have[key] == 4:
+            use(lax.rem(x + key[0], 2), lax.rem(z + key[1], nz))
+
+    def use(xk, zk):
         at = lanes(xk, zk)
         wt = jnp.concatenate(
             [G[0, xk, zk].reshape(half, rows), G[1, xk, zk].reshape(half, rows)], axis=0
@@ -174,66 +190,65 @@
         ACC[...] += part
         back = factor * jnp.dot(cot, wt, preferred_element_type=F32)
         scaled = x_ref[:, at].astype(F32) * RSTD[...]
-        GA[pl.ds(zk * 2 + xk, 1), :] = jnp.sum(back * scaled, axis=0, keepdims=True)
+        GA[zk * 2 + xk] = jnp.sum(back * scaled, axis=0, keepdims=True)
 
     ACC[...] = jnp.zeros_like(ACC)
-    for k in range(chunks):
-        stage_term(k)
-        if k >= 1:
-            stage_core(k - 1)
-    stage_core(chunks - 1)
-    stage_y(0)
-    stage_y(1)
-    use(nz - 1)
-    forward_x(nz - 1)
-    done = 2
-    for j in reversed(range(nz - 1)):
-        stage_y(done)
-        forward_z(j)
-        use(nz + nz - 1) if j == nz - 2 else forward_x(j + 1)
-        done += 1
-    for j in reversed(range(nz - 1)):
-        if done < chunks:
-            stage_y(done)
-            done += 1
-        use(j)
-    forward_x(0)
-    while done < chunks:
-        stage_y(done)
-        done += 1
-    for j in reversed(range(nz - 1)):
-        use(nz + j)
-
-    send(GA, GR.at[0], ga_s.at[0], ga_r.at[0], core_dev)
+    count = dict(T=0, C=0, Y=0)
+    stages = dict(T=stage_term, C=stage_core, Y=stage_y)
+    for letter in PLAN + "P" * (4 * chunks) + "TTTTCCCCYYYY" * 2:
+        if letter == "P":
+            if waiting:
+                pump()
+        elif count[letter] < chunks:
+            stages[letter](count[letter])
+            count[letter] += 1
+
+    row = x * 4 + y * 2 + c
+    for q, (dev, other) in enumerate(group):
+        send(GA.at[other], GR.at[q], ga_s.at[q], ga_r.at[q], dev)
     out = lax.dot_general(
         (factor * ACC[...]).astype(BF16), perm, (((1,), (1,)), ((), ())), preferred_element_type=F32
     )
     proj_ref[...] = out.astype(BF16)
-    arrived(GR.at[0], ga_s.at[0], ga_r.at[0], core_dev)
-    GB[0] = GA[...] + GR[0]
-    send(GB.at[0], GR.at[1], ga_s.at[1], ga_r.at[1], y_dev)
-    arrived(GR.at[1], ga_s.at[1], ga_r.at[1], y_dev)
-    GB[1] = GB[0] + GR[1]
-    send(GB.at[1], GR.at[2], ga_s.at[2], ga_r.at[2], x_dev)
-    arrived(GR.at[2], ga_s.at[2], ga_r.at[2], x_dev)
-    GZ[z] = GB[1] + GR[2]
+    part = GA[row]
+    for q, (dev, _) in enumerate(group):
+        arrived(GR.at[q], ga_s.at[q], ga_r.at[q], dev)
+        part = part + GR[q]
+    GZ[z] = part
     for j in range(nz - 1):
-        send(GZ.at[z], GZ.at[z], ga_s.at[3 + j], ga_r.at[3 + j], z_dev[j])
+        send(GZ.at[z], GZ.at[z], gt_s.at[j], gt_r.at[j], z_dev[j])
 
     grad = OWN[...]
     for j in range(nz - 1):
         arrived(RZ.at[j], rz_s.at[j], rz_r.at[j], z_dev[j])
         grad = grad + RZ[j].astype(F32)
-    nw_ref[...], n1_ref[...], n2_ref[...] = adam(grad, w_ref[...], m1_ref[...], m2_ref[...])
+    grad_ref[...] = grad
 
     for j in range(nz - 1):
-        arrived(GZ.at[z_from[j]], ga_s.at[3 + j], ga_r.at[3 + j], z_dev[j])
+        arrived(GZ.at[z_from[j]], gt_s.at[j], gt_r.at[j], z_dev[j])
     total = GZ[0]
     for j in range(1, nz):
         total = total + GZ[j]
-    gg_ref[...] = total
+    GB[row] = total
+    for q, (dev, _) in enumerate(group):
+        send(GB.at[row], GB.at[row], gb_s.at[q], gb_r.at[q], dev)
+    for q, (dev, other) in enumerate(group):
+        arrived(GB.at[other], gb_s.at[q], gb_r.at[q], dev)
+    for r in range(chunks):
+        gg_ref[r : r + 1, :] = GB[r]
     for d in sends:
         d.wait_send()
+
+
+def finish(p_ref, g_ref, grad_ref, w_ref, m1_ref, m2_ref, proj_ref, gg_ref, nw_ref, n1_ref, n2_ref):
+    proj_ref[...] = p_ref[...]
+    per = g_ref.shape[1] // 128
+    for r in range(gg_ref.shape[0]):
+        at = (r % per) * 128
+        gg_ref[r : r + 1, :] = g_ref[r // per : r // per + 1, at : at + 128]
+    nw_ref[...], n1_ref[...], n2_ref[...] = adam(
+        grad_ref[...], w_ref[...], m1_ref[...], m2_ref[...]
+    )
 
 
 def per_device(nz, inputs, norm_gain, cotangent, weights, first_moment, second_moment):
@@ -244,18 +259,14 @@
     dma = lambda *n: pltpu.SemaphoreType.DMA(n)
     sd = jax.ShapeDtypeStruct
     block = (cols, rows)
-    outs = pl.pallas_call(
+    weights, first_moment, second_moment = weights.T, first_moment.T, second_moment.T
+    projected, gains, grad = pl.pallas_call(
         functools.partial(kernel, nz),
-        out_shape=(
-            sd((tok, 4 * cols), BF16),
-            sd((chunks, rows), F32),
-            sd(block, BF16),
-            sd(block, BF16),
-            sd(block, BF16),
-        ),
-        in_specs=[vm] * 6,
-        out_specs=(vm,) * 5,
+        out_shape=(sd((tok, 4 * cols), BF16), sd((chunks, rows), F32), sd(block, F32)),
+        in_specs=[vm] * 4,
+        out_specs=(vm,) * 3,
         scratch_shapes=[
+            pltpu.VMEM((1, width), F32),
             pltpu.VMEM((2, 2, nz, 2) + block, BF16),
             pltpu.VMEM((chunks, 2, 2) + block, BF16),
             pltpu.VMEM((chunks, 2) + block, BF16),
@@ -269,20 +280,28 @@
             pltpu.VMEM((chunks, tok, rows), BF16),
             pltpu.VMEM((tok, 1), F32),
             pltpu.VMEM((tok, 4 * cols), F32),
-            pltpu.VMEM((chunks, rows), F32),
-            pltpu.VMEM((2, chunks, rows), F32),
-            pltpu.VMEM((3, chunks, rows), F32),
-            pltpu.VMEM((nz, chunks, rows), F32),
-            pltpu.SemaphoreType.DMA, pltpu.SemaphoreType.DMA,
-            dma(nz - 1), dma(nz - 1), dma(nz), dma(nz), dma(chunks), dma(chunks),
+            pltpu.VMEM((chunks, 1, rows), F32),
+            pltpu.VMEM((chunks, 1, rows), F32),
+            pltpu.VMEM((7, 1, rows), F32),
+            pltpu.VMEM((nz, 1, rows), F32),
+            dma(4 * chunks - 1), dma(4 * chunks - 1),
             dma(chunks), dma(chunks), dma(chunks), dma(chunks),
-            dma(nz), dma(nz), dma(nz - 1), dma(nz - 1), dma(nz + 2), dma(nz + 2),
+            dma(nz), dma(nz), dma(nz - 1), dma(nz - 1), dma(7), dma(7),
+            dma(nz - 1), dma(nz - 1), dma(7), dma(7),
         ],
         compiler_params=pltpu.CompilerParams(
             collective_id=0, has_side_effects=True, vmem_limit_bytes=56 * 2**20
         ),
-    )(inputs, norm_gain.reshape(1, width), cotangent, weights.T, first_moment.T, second_moment.T)
-    projected, gain_grad, new_weights, first, second = outs
+    )(inputs, norm_gain.reshape(width // 128, 128), cotangent, weights)
+    projected, gain_grad, new_weights, first, second = pl.pallas_call(
+        finish,
+        out_shape=(
+            sd((tok, 4 * cols), BF16), sd((width // 128, 128), F32),
+            sd(block, BF16), sd(block, BF16), sd(block, BF16),
+        ),
+        in_specs=[vm] * 6,
+        out_specs=(vm,) * 5,
+    )(projected, gains, grad, weights, first_moment, second_moment)
     return projected, gain_grad.reshape(width), new_weights.T, first.T, second.T
 
 
@@ -292,7 +311,7 @@
     def body(inputs, norm_gain, cotangent, weights, first_moment, second_moment):
         args = (inputs, norm_gain, cotangent, weights, first_moment, second_moment)
         rows, cols = weights.shape
-        if node == 4 and dp in (4, 6, 8) and rows % 128 == 0 and cols % 16 == 0:
+        if node == 4 and dp == 8 and rows % 128 == 0 and cols % 16 == 0:
             return per_device(dp // 2, *args)
         return plain(*args)
 

time: 64.2 us -> 53.2 us (0.83)
  local copies, waits for them, and re-layouts: 8.8 us -> 0 us
  Pallas kernels: 54.4 us -> 52.5 us
    unnamed x4 -> x0, local copies, waits for them, and re-layouts: 6 us -> none
    pallas_call x1, Pallas kernels: 54.4 us -> 50.4 us  [per_device(): pl.pallas_call(functools.partial(kernel, nz), out_shape=(sd((tok, 4 * col...]
    reshape x2 -> x0, local copies, waits for them, and re-layouts: 2.81 us -> none  [the longest x1 1.42 us: per_device(): gain_grad.reshape(width)]
    pallas_call x0 -> x1, Pallas kernels: none -> 2.04 us  [per_device(): pl.pallas_call(finish, out_shape=(sd((tok, 4 * cols), BF16), sd((width //...]
where the time goes in v2:
time: 53.2 us; the launch traced here: 53.1 us
  Pallas kernels  52.5 us (99%)
  between operations  0.64 us (1%)
    pallas_call x1, Pallas kernels, per_device(): pl.pallas_call(functools.partial(kernel, nz), out_shape=(sd((tok, 4 * col...  50.4 us
    pallas_call x1, Pallas kernels, per_device(): pl.pallas_call(finish, out_shape=(sd((tok, 4 * cols), BF16), sd((width //...  2.04 us

profile of v2, /device:TPU:0, one launch (start us, length us, event | category | flops | bytes accessed | tf_op | source)
XLA Modules:
  0.0 53.1 jit_solution(12536832642300704003)
XLA Ops:
  0.6 50.4 %shard_map.101 = (bf16[136,128]{1,0:T(8,128)(2,1)}, f32[8,1536]{1,0:T(8,128)}, f32[32,1536]{1,0:T(8,128)}) custom-call(bf16[136,12288]{1,0:T(8,128)(2,1)} %x_ref.1, bf16[96,128]{1,0:T(8,128)(2,1)} %bitcast.12, bf16[136,128]{1,0:T(8,128)(2,1)} %cot_ref.1, bf16[32,1536]{1,0:T(8,128)(2,1)} %bitcast.8), custom_call_target="tpu_custom_call" | custom-call | tf_op jit(solution)/shard_map/pallas_call | solution.py:263
  51.0 2.0 %shard_map.102 = (bf16[136,128]{1,0:T(8,128)(2,1)}, f32[96,128]{1,0:T(8,128)}, bf16[32,1536]{1,0:T(8,128)(2,1)}, bf16[32,1536]{1,0:T(8,128)(2,1)}, bf16[32,1536]{1,0:T(8,128)(2,1)}) custom-call(bf16[136,128]{1,0:T(8,128)(2,1)} %get-tuple-element.13.p_ref, f32[8,1536]{1,0:T(8,128)} %get-tuple-element.14.g_ref, f32[32,1536]{1,0:T(8,128)} %get-tuple-element.15.grad_ref, ...), custom_call_target="tpu_custom_call" | custom-call | tf_op jit(solution)/shard_map/pallas_call | solution.py:296

commit v3 on v2

--- a/solution.py
+++ b/solution.py
@@ -9,7 +9,7 @@
 
 STEP = 20
 ORDER = "yzxc"
-PLAN = "TTCP" + "TCYP" * 6 + "CP" + "YPPP" * 8
+PLAN = "PTTC" + "TCYP" * 6 + "CP" + "YPPP" * 8
 MESH = pl.DeviceIdType.MESH
 F32 = jnp.float32
 BF16 = jnp.bfloat16

time: 53.2 us -> 57 us (1.071)
  Pallas kernels: 52.5 us -> 56.2 us
    pallas_call x1, Pallas kernels: 50.4 us -> 54.2 us  [per_device(): pl.pallas_call(functools.partial(kernel, nz), out_shape=(sd((tok, 4 * col...]
where the time goes in v3:
time: 57 us; the launch traced here: 56.9 us
  Pallas kernels  56.2 us (99%)
  between operations  0.64 us (1%)
    pallas_call x1, Pallas kernels, per_device(): pl.pallas_call(functools.partial(kernel, nz), out_shape=(sd((tok, 4 * col...  54.2 us
    pallas_call x1, Pallas kernels, per_device(): pl.pallas_call(finish, out_shape=(sd((tok, 4 * cols), BF16), sd((width //...  2.04 us

profile of v3, /device:TPU:0, one launch (start us, length us, event | category | flops | bytes accessed | tf_op | source)
XLA Modules:
  0.0 56.9 jit_solution(13770884405030488812)
XLA Ops:
  0.6 54.2 %shard_map.101 = (bf16[136,128]{1,0:T(8,128)(2,1)}, f32[8,1536]{1,0:T(8,128)}, f32[32,1536]{1,0:T(8,128)}) custom-call(bf16[136,12288]{1,0:T(8,128)(2,1)} %x_ref.1, bf16[96,128]{1,0:T(8,128)(2,1)} %bitcast.12, bf16[136,128]{1,0:T(8,128)(2,1)} %cot_ref.1, bf16[32,1536]{1,0:T(8,128)(2,1)} %bitcast.8), custom_call_target="tpu_custom_call" | custom-call | tf_op jit(solution)/shard_map/pallas_call | solution.py:263
  54.8 2.0 %shard_map.102 = (bf16[136,128]{1,0:T(8,128)(2,1)}, f32[96,128]{1,0:T(8,128)}, bf16[32,1536]{1,0:T(8,128)(2,1)}, bf16[32,1536]{1,0:T(8,128)(2,1)}, bf16[32,1536]{1,0:T(8,128)(2,1)}) custom-call(bf16[136,128]{1,0:T(8,128)(2,1)} %get-tuple-element.13.p_ref, f32[8,1536]{1,0:T(8,128)} %get-tuple-element.14.g_ref, f32[32,1536]{1,0:T(8,128)} %get-tuple-element.15.grad_ref, ...), custom_call_target="tpu_custom_call" | custom-call | tf_op jit(solution)/shard_map/pallas_call | solution.py:296
